TPU v7x, 128 devices: a whole 4x4x4 slice. The times are simulated.
128 devices in a mesh: rep: 16 (over x_lo, z, core), shard: 8 (over x_hi, y).
Axes of the slice: x: 4 (x_hi: 2, x_lo: 2; x = x_hi * 2 + x_lo), y: 4, z: 4, core: 2. Of those that a mesh axis runs over, the one named last changes fastest.
Arguments:
- latents: bfloat16 [16, 1024, 1024], P('rep', 'shard'), may hold values from -6 to 6
- cond: bfloat16 [16, 1024], P('rep'), may hold values from -6 to 6
- cotangent: bfloat16 [16, 1024, 1024], P('rep', 'shard'), may hold values from -6 to 6
- w_qkv: bfloat16 [1024, 3072], P('shard'), may hold values from -0.1875 to 0.1875
- bias_qv: bfloat16 [2048], P('shard'), may hold values from -3 to 3
- w_proj: bfloat16 [1024, 1024], P('shard'), may hold values from -1 to 1
- b_proj: bfloat16 [1024], P('shard'), may hold values from -3 to 3
- w_fc1: bfloat16 [1024, 4096], P('shard'), may hold values from -0.1875 to 0.1875
- b_fc1: bfloat16 [4096], P('shard'), may hold values from -3 to 3
- w_fc2: bfloat16 [4096, 1024], P('shard'), may hold values from -0.09375 to 0.09375
- b_fc2: bfloat16 [1024], P('shard'), may hold values from -3 to 3
- w_ada: bfloat16 [1024, 6144], P('shard'), may hold values from -0.1875 to 0.1875
- b_ada: bfloat16 [6144], P('shard'), may hold values from -3 to 3
Outputs:
- output: bfloat16 [16, 1024, 1024], P('rep', 'shard')
- grad_latents: bfloat16 [16, 1024, 1024], P('rep', 'shard')
- grad_cond: float32 [16, 1024], P('rep')
- grad_w_qkv: float32 [1024, 3072], P('shard')
- grad_bias_qv: float32 [2048], P('shard')
- grad_w_proj: float32 [1024, 1024], P('shard')
- grad_b_proj: float32 [1024], P('shard')
- grad_w_fc1: float32 [1024, 4096], P('shard')
- grad_b_fc1: float32 [4096], P('shard')
- grad_w_fc2: float32 [4096, 1024], P('shard')
- grad_b_fc2: float32 [1024], P('shard')
- grad_w_ada: float32 [1024, 6144], P('shard')
- grad_b_ada: float32 [6144], P('shard')
All inputs are finite; a program needn't handle non-finite values.
Results may differ from a plain program's by a relative error of at most 0.025.
Values may be sent and summed in bfloat16 or wider, within the bound.
No kernel may reach another device: no remote copies, remote signals or barrier semaphores. Data moves between devices by JAX's collectives and lax.ppermute only.
A program may use at most 192 MiB of HBM per device.

v0:
```python
import jax
import jax.numpy as jnp
from jax import lax
from jax.sharding import PartitionSpec as P

HEAD = 64


epsilon = 1e-06
highest = lax.Precision.HIGHEST


def as_sent(value):
    return jax.tree.map(lambda a: a.astype(jnp.bfloat16) if a.dtype == jnp.float32 else a, value)


def layer_norm(values):
    centered = values - jnp.mean(values, axis=-1, keepdims=True)
    variance = jnp.mean(centered * centered, axis=-1, keepdims=True)
    return centered * lax.rsqrt(variance + epsilon)


def sigmoid_linear(values):
    return values / (1.0 + jnp.exp(-values))


def gelu_tanh(values):
    return (
        0.5
        * values
        * (1.0 + jnp.tanh(0.7978845608028654 * (values + 0.044715 * values * values * values)))
    )


def project(left, right):
    return jnp.einsum("lrd,de->lre", left, right, preferred_element_type=jnp.float32)


def project_back(left, right):
    return jnp.einsum("lre,de->lrd", left, right, preferred_element_type=jnp.float32)


def on_device(
    latents,
    cond,
    cotangent,
    w_qkv,
    bias_qv,
    w_proj,
    b_proj,
    w_fc1,
    b_fc1,
    w_fc2,
    b_fc2,
    w_ada,
    b_ada,
):
    count_lat = latents.shape[0]
    rows = latents.shape[1]
    features = latents.shape[2]
    heads = features // HEAD
    score_scale = HEAD ** (-0.5)
    gathered = (
        lax.all_gather(w_qkv, "shard", axis=0, tiled=True),
        lax.all_gather(bias_qv, "shard", axis=0, tiled=True),
        lax.all_gather(w_proj, "shard", axis=0, tiled=True),
        lax.all_gather(b_proj, "shard", axis=0, tiled=True),
        lax.all_gather(w_fc1, "shard", axis=0, tiled=True),
        lax.all_gather(b_fc1, "shard", axis=0, tiled=True),
        lax.all_gather(w_fc2, "shard", axis=0, tiled=True),
        lax.all_gather(b_fc2, "shard", axis=0, tiled=True),
        lax.all_gather(w_ada, "shard", axis=0, tiled=True),
        lax.all_gather(b_ada, "shard", axis=0, tiled=True),
    )
    whole_qkv = gathered[0]
    whole_proj = gathered[2]
    whole_fc1 = gathered[4]
    whole_fc2 = gathered[6]
    whole_ada = gathered[8]
    bias_wide = gathered[1].astype(jnp.float32)
    stream = latents.astype(jnp.float32)
    cond_value = cond.astype(jnp.float32)
    cond_silu, silu_pull = jax.vjp(sigmoid_linear, cond_value)
    cond_low = cond_silu.astype(jnp.bfloat16)
    modulation = jnp.dot(cond_low, whole_ada, preferred_element_type=jnp.float32) + gathered[
        9
    ].astype(jnp.float32)
    shift_first, scale_first, gate_first, shift_second, scale_second, gate_second = jnp.split(
        modulation[:, None, :], 6, axis=2
    )
    norm_first, first_pull = jax.vjp(layer_norm, stream)
    attend_in = (norm_first * (1.0 + scale_first) + shift_first).astype(jnp.bfloat16)
    packed = project(attend_in, whole_qkv)
    queries = (packed[:, :, :features] + bias_wide[:features]).astype(jnp.bfloat16)
    keyset = packed[:, :, features : 2 * features].astype(jnp.bfloat16)
    valueset = (packed[:, :, 2 * features :] + bias_wide[features:]).astype(jnp.bfloat16)
    key_all, value_all = (
        lax.all_gather(keyset, "shard", axis=1, tiled=True),
        lax.all_gather(valueset, "shard", axis=1, tiled=True),
    )
    length = key_all.shape[1]
    query_heads = queries.reshape(count_lat, rows, heads, HEAD)
    key_heads = key_all.reshape(count_lat, length, heads, HEAD)
    value_heads = value_all.reshape(count_lat, length, heads, HEAD)
    scores = (
        jnp.einsum("lqhe,lkhe->lhqk", query_heads, key_heads, preferred_element_type=jnp.float32)
        * score_scale
    )
    row_peak = jnp.max(scores, axis=-1, keepdims=True)
    powered = jnp.exp(scores - row_peak)
    row_total = jnp.sum(powered, axis=-1, keepdims=True)
    attention = powered / row_total
    log_total = row_peak + jnp.log(row_total)
    mixed_heads = jnp.einsum(
        "lhqk,lkhe->lqhe",
        attention.astype(jnp.bfloat16),
        value_heads,
        preferred_element_type=jnp.float32,
    )
    mixed_low = mixed_heads.reshape(count_lat, rows, features).astype(jnp.bfloat16)
    branch = project(mixed_low, whole_proj) + gathered[3].astype(jnp.float32)
    middle = stream + gate_first * branch
    norm_second, second_pull = jax.vjp(layer_norm, middle)
    feed_in = (norm_second * (1.0 + scale_second) + shift_second).astype(jnp.bfloat16)
    hidden = project(feed_in, whole_fc1) + gathered[5].astype(jnp.float32)
    active_value, gelu_pull = jax.vjp(gelu_tanh, hidden)
    active_low = active_value.astype(jnp.bfloat16)
    branch_second = project(active_low, whole_fc2) + gathered[7].astype(jnp.float32)
    output = (middle + gate_second * branch_second).astype(jnp.bfloat16)
    regathered = (
        lax.all_gather(w_qkv, "shard", axis=0, tiled=True),
        lax.all_gather(w_proj, "shard", axis=0, tiled=True),
        lax.all_gather(w_fc1, "shard", axis=0, tiled=True),
        lax.all_gather(w_fc2, "shard", axis=0, tiled=True),
        lax.all_gather(w_ada, "shard", axis=0, tiled=True),
    )
    back_qkv = regathered[0]
    back_proj = regathered[1]
    back_fc1 = regathered[2]
    back_fc2 = regathered[3]
    back_ada = regathered[4]
    upstream = cotangent.astype(jnp.float32)
    grad_gate_second = jnp.sum(upstream * branch_second, axis=1)
    grad_branch_second = (upstream * gate_second).astype(jnp.bfloat16)
    grad_active = project_back(grad_branch_second, back_fc2)
    grad_hidden = gelu_pull(grad_active)[0].astype(jnp.bfloat16)
    grad_feed = project_back(grad_hidden, back_fc1)
    grad_scale_second = jnp.sum(grad_feed * norm_second, axis=1)
    grad_shift_second = jnp.sum(grad_feed, axis=1)
    grad_middle = upstream + second_pull(grad_feed * (1.0 + scale_second))[0]
    grad_gate_first = jnp.sum(grad_middle * branch, axis=1)
    grad_branch = (grad_middle * gate_first).astype(jnp.bfloat16)
    grad_mixed = (
        project_back(grad_branch, back_proj)
        .astype(jnp.bfloat16)
        .reshape(count_lat, rows, heads, HEAD)
    )
    again_scores = (
        jnp.einsum("lqhe,lkhe->lhqk", query_heads, key_heads, preferred_element_type=jnp.float32)
        * score_scale
    )
    again_probs = jnp.exp(again_scores - log_total)
    grad_probs = jnp.einsum(
        "lqhe,lkhe->lhqk", grad_mixed, value_heads, preferred_element_type=jnp.float32
    )
    grad_value = jnp.einsum(
        "lhqk,lqhe->lkhe",
        again_probs.astype(jnp.bfloat16),
        grad_mixed,
        preferred_element_type=jnp.float32,
    )
    row_delta = jnp.sum(again_probs * grad_probs, axis=-1, keepdims=True)
    grad_scores = (again_probs * (grad_probs - row_delta)).astype(jnp.bfloat16)
    grad_query = (
        (
            jnp.einsum(
                "lhqk,lkhe->lqhe", grad_scores, key_heads, preferred_element_type=jnp.float32
            )
            * score_scale
        )
        .reshape(count_lat, rows, features)
        .astype(jnp.bfloat16)
    )
    grad_key = (
        jnp.einsum("lhqk,lqhe->lkhe", grad_scores, query_heads, preferred_element_type=jnp.float32)
        * score_scale
    )
    key_owned, value_owned = (
        lax.psum_scatter(
            grad_key.reshape(count_lat, length, features).astype(jnp.bfloat16),
            "shard",
            scatter_dimension=1,
            tiled=True,
        ).astype(jnp.float32),
        lax.psum_scatter(
            grad_value.reshape(count_lat, length, features).astype(jnp.bfloat16),
            "shard",
            scatter_dimension=1,
            tiled=True,
        ).astype(jnp.float32),
    )
    key_low = key_owned.astype(jnp.bfloat16)
    value_low = value_owned.astype(jnp.bfloat16)
    grad_packed = jnp.concatenate([grad_query, key_low, value_low], axis=2)
    grad_attend = project_back(grad_packed, back_qkv)
    grad_scale_first = jnp.sum(grad_attend * norm_first, axis=1)
    grad_shift_first = jnp.sum(grad_attend, axis=1)
    grad_stream = grad_middle + first_pull(grad_attend * (1.0 + scale_first))[0]
    grad_latents = grad_stream.astype(jnp.bfloat16)
    grad_modulation = jnp.concatenate(
        [
            grad_shift_first,
            grad_scale_first,
            grad_gate_first,
            grad_shift_second,
            grad_scale_second,
            grad_gate_second,
        ],
        axis=1,
    )
    cond_wide = cond_low.astype(jnp.float32)
    cond_term = jnp.einsum(
        "lm,dm->ld",
        grad_modulation,
        back_ada,
        precision=highest,
        preferred_element_type=jnp.float32,
    )
    cond_total = lax.psum(cond_term, "shard")
    grad_cond = silu_pull(cond_total)[0]
    term_qkv = jnp.einsum("lrc,lre->ce", attend_in, grad_packed, preferred_element_type=jnp.float32)
    term_proj = jnp.einsum(
        "lrc,lre->ce", mixed_low, grad_branch, preferred_element_type=jnp.float32
    )
    term_fc1 = jnp.einsum("lrc,lre->ce", feed_in, grad_hidden, preferred_element_type=jnp.float32)
    pieces = [term_qkv, term_proj, term_fc1]
    pieces.append(jnp.dot(cond_wide.T, grad_modulation, precision=highest))
    row_owned = lax.psum_scatter(
        jnp.concatenate(pieces, axis=1).astype(jnp.bfloat16),
        "shard",
        scatter_dimension=0,
        tiled=True,
    ).astype(jnp.float32)
    units = active_low.shape[2]
    second_owned = lax.psum_scatter(
        jnp.einsum(
            "lrc,lre->ce", active_low, grad_branch_second, preferred_element_type=jnp.float32
        ).astype(jnp.bfloat16),
        "shard",
        scatter_dimension=0,
        tiled=True,
    )
    bias_query = jnp.sum(grad_query.astype(jnp.float32), axis=(0, 1))
    bias_value = jnp.sum(value_low.astype(jnp.float32), axis=(0, 1))
    base_terms = (
        jnp.concatenate([bias_query, bias_value], axis=0),
        jnp.sum(grad_branch.astype(jnp.float32), axis=(0, 1)),
        jnp.sum(grad_hidden.astype(jnp.float32), axis=(0, 1)),
        jnp.sum(grad_branch_second.astype(jnp.float32), axis=(0, 1)),
    )
    bias_terms = base_terms + (jnp.sum(grad_modulation, axis=0),)
    bias_owned = jax.tree.map(
        lambda part: part.astype(jnp.float32),
        lax.psum_scatter(as_sent(bias_terms), "shard", scatter_dimension=0, tiled=True),
    )
    wide_qkv = 3 * features
    owned_qkv = row_owned[:, :wide_qkv]
    owned_proj = row_owned[:, wide_qkv : wide_qkv + features]
    owned_fc1 = row_owned[:, wide_qkv + features : wide_qkv + features + units]
    owned_ada = row_owned[:, wide_qkv + features + units :]
    owned_ada_bias = bias_owned[4]
    totals = (
        lax.psum(owned_qkv.astype(jnp.bfloat16), "rep").astype(jnp.float32),
        lax.psum(bias_owned[0].astype(jnp.bfloat16), "rep").astype(jnp.float32),
        lax.psum(owned_proj.astype(jnp.bfloat16), "rep").astype(jnp.float32),
        lax.psum(bias_owned[1].astype(jnp.bfloat16), "rep").astype(jnp.float32),
        lax.psum(owned_fc1.astype(jnp.bfloat16), "rep").astype(jnp.float32),
        lax.psum(bias_owned[2].astype(jnp.bfloat16), "rep").astype(jnp.float32),
        lax.psum(second_owned, "rep").astype(jnp.float32),
        lax.psum(bias_owned[3].astype(jnp.bfloat16), "rep").astype(jnp.float32),
        lax.psum(owned_ada.astype(jnp.bfloat16), "rep").astype(jnp.float32),
        lax.psum(owned_ada_bias.astype(jnp.bfloat16), "rep").astype(jnp.float32),
    )
    return (
        output,
        grad_latents,
        grad_cond,
        totals[0],
        totals[1],
        totals[2],
        totals[3],
        totals[4],
        totals[5],
        totals[6],
        totals[7],
        totals[8],
        totals[9],
    )


def solution(mesh):
    placed = (
        P("rep", "shard", None),
        P("rep", None),
        P("rep", "shard", None),
        P("shard", None),
        P("shard"),
        P("shard", None),
        P("shard"),
        P("shard", None),
        P("shard"),
        P("shard", None),
        P("shard"),
        P("shard", None),
        P("shard"),
    )
    return jax.shard_map(
        on_device,
        mesh=mesh,
        in_specs=placed,
        out_specs=(
            P("rep", "shard", None),
            P("rep", "shard", None),
            P("rep", None),
            P("shard", None),
            P("shard"),
            P("shard", None),
            P("shard"),
            P("shard", None),
            P("shard"),
            P("shard", None),
            P("shard"),
            P("shard", None),
            P("shard"),
        ),
        check_vma=False,
    )
```

profile of v0, /device:TPU:1, one launch (start us, length us, event | category | flops | bytes accessed | tf_op | source)
XLA Modules:
  0.0 1435.0 jit_solution(15415909941565255366)
XLA Ops:
  10.1 29.1 %all-gather = bf16[8,1,768]{2,1,0:T(2,128)(2,1)S(1)} all-gather(bf16[1,1,768]{2,1,0:T(2,128)(2,1)S(1)} %reshape.411), channel_id=1, replica_groups=mesh['rep'=16,'shard'=8] {'shard'}, dimensions={0}, use_global_device_ids=true | all-gather | bytes 13824 | tf_op jit(solution)/shard_map/all_gather | solution.py:73
  39.2 19.1 %all-gather.1 = bf16[8,1,256]{2,1,0:T(2,128)(2,1)S(1)} all-gather(bf16[1,1,256]{2,1,0:T(2,128)(2,1)S(1)} %reshape.413), channel_id=1, replica_groups=mesh['rep'=16,'shard'=8] {'shard'}, dimensions={0}, use_global_device_ids=true | all-gather | bytes 4608 | tf_op jit(solution)/shard_map/all_gather | solution.py:65
  60.6 97.7 %all-gather.13.cloned.1.call-done = bf16[1024,6144]{1,0:T(8,128)(2,1)} async-done(((bf16[128,6144]{1,0:T(8,128)(2,1)}), bf16[1024,6144]{1,0:T(8,128)(2,1)}) %all-gather.13.cloned.1.call-update) | async-done | bytes 12582928 | tf_op jit(solution)/shard_map/all_gather | solution.py:72
  158.2 6.3 fusion.53
  164.6 82.7 %all-gather.15.cloned.1.call-done = bf16[1024,3072]{1,0:T(8,128)(2,1)} async-done(((bf16[128,3072]{1,0:T(8,128)(2,1)}), bf16[1024,3072]{1,0:T(8,128)(2,1)}) %all-gather.15.cloned.1.call-update) | async-done | bytes 6291472 | tf_op jit(solution)/shard_map/all_gather | solution.py:64
  254.8 15.0 %all-gather.2 = bf16[8,1,128]{2,1,0:T(2,128)(2,1)S(1)} all-gather(bf16[1,1,128]{2,1,0:T(2,128)(2,1)S(1)} %bitcast.211), channel_id=1, replica_groups=mesh['rep'=16,'shard'=8] {'shard'}, dimensions={0}, use_global_device_ids=true | all-gather | bytes 2304 | tf_op jit(solution)/shard_map/all_gather | solution.py:67
  269.8 25.5 %all-gather.3 = bf16[8,1,512]{2,1,0:T(2,128)(2,1)S(1)} all-gather(bf16[1,1,512]{2,1,0:T(2,128)(2,1)S(1)} %reshape.417), channel_id=1, replica_groups=mesh['rep'=16,'shard'=8] {'shard'}, dimensions={0}, use_global_device_ids=true | all-gather | bytes 9216 | tf_op jit(solution)/shard_map/all_gather | solution.py:69
  295.5 8.5 all-gather.17.cloned.1.call-done
  308.0 50.7 %all-gather.19.cloned.1.call-done = bf16[1,1024,1024]{2,1,0:T(8,128)(2,1)} async-done(((bf16[1,128,1024]{2,1,0:T(8,128)(2,1)}), bf16[1,1024,1024]{2,1,0:T(8,128)(2,1)}) %all-gather.19.cloned.1.call-update) | async-done | bytes 2097168 | tf_op jit(solution)/shard_map/all_gather | solution.py:98
  369.0 43.7 %all-gather.21.cloned.1.call-done = bf16[1024,1024]{1,0:T(8,128)(2,1)} async-done(((bf16[128,1024]{1,0:T(8,128)(2,1)}), bf16[1024,1024]{1,0:T(8,128)(2,1)}) %all-gather.21.cloned.1.call-update) | async-done | bytes 2097168 | tf_op jit(solution)/shard_map/all_gather | solution.py:66
  415.8 104.0 %all-gather.23.cloned.1.call-done = bf16[1024,4096]{1,0:T(8,128)(2,1)} async-done(((bf16[128,4096]{1,0:T(8,128)(2,1)}), bf16[1024,4096]{1,0:T(8,128)(2,1)}) %all-gather.23.cloned.1.call-update) | async-done | bytes 8388624 | tf_op jit(solution)/shard_map/all_gather | solution.py:68
  519.8 6.1 convolution_add_fusion
  525.9 101.2 %all-gather.25.cloned.1.call-done = bf16[4096,1024]{1,0:T(8,128)(2,1)} async-done(((bf16[512,1024]{1,0:T(8,128)(2,1)}), bf16[4096,1024]{1,0:T(8,128)(2,1)}) %all-gather.25.cloned.1.call-update) | async-done | bytes 8388624 | tf_op jit(solution)/shard_map/all_gather | solution.py:70
  627.1 8.3 fusion.74
  643.7 6.7 fusion.13
  650.4 10.9 copy.47
  665.9 6.8 multiply_reduce_fusion
  681.5 11.0 copy.45
  697.0 14.9 %all-gather.4 = bf16[8,1,128]{2,1,0:T(2,128)(2,1)S(1)} all-gather(bf16[1,1,128]{2,1,0:T(2,128)(2,1)S(1)} %bitcast.212), channel_id=1, replica_groups=mesh['rep'=16,'shard'=8] {'shard'}, dimensions={0}, use_global_device_ids=true | all-gather | bytes 2304 | tf_op jit(solution)/shard_map/all_gather | solution.py:71
  728.6 9.0 reduce-scatter.15.cloned.1.call-done
  739.6 75.9 %reduce-scatter.13.cloned.1.call-done = bf16[128,1024]{1,0:T(8,128)(2,1)} async-done(((bf16[1024,1024]{1,0:T(8,128)(2,1)}), bf16[128,1024]{1,0:T(8,128)(2,1)}) %reduce-scatter.13.cloned.1.call-update) | async-done | bytes 262160
  822.9 6.2 fusion.28
  831.6 6.2 fusion.30
  837.9 7.5 multiply_convert_fusion
  845.4 19.0 %pad_maximum_fusion = bf16[1024,14336]{1,0:T(8,128)(2,1)} fusion(bf16[1024,6144]{1,0:T(8,128)(2,1)} %multiply_convert_fusion, bf16[1024,4096]{1,0:T(8,128)(2,1)} %convolution_convert_fusion.1, bf16[1024,1024]{1,0:T(8,128)(2,1)S(1)} %copy-done.5, bf16[1024,3072]{1,0:T(8,128)(2,1)} %convolution_convert_fusion.2), kind=kLoop, calls=%fused_computation | loop fusion | flops 117440512 | bytes 58720256 | tf_op jit(solution)/shard_map/concatenate | solution.py:239
  871.0 295.1 %reduce-scatter.9.cloned.1.call-done = bf16[128,14336]{1,0:T(8,128)(2,1)} async-done(((bf16[1024,14336]{1,0:T(8,128)(2,1)}), bf16[128,14336]{1,0:T(8,128)(2,1)}) %reduce-scatter.9.cloned.1.call-update) | async-done | bytes 3670032 | tf_op jit(solution)/shard_map/reduce_scatter | solution.py:238
  1174.8 108.6 %reduce-scatter.11.cloned.1.call-done = bf16[512,1024]{1,0:T(8,128)(2,1)} async-done(((bf16[4096,1024]{1,0:T(8,128)(2,1)}), bf16[512,1024]{1,0:T(8,128)(2,1)}) %reduce-scatter.11.cloned.1.call-update) | async-done | bytes 1048592 | tf_op jit(solution)/shard_map/reduce_scatter | solution.py:245
  1286.7 30.5 %all-reduce.7 = (bf16[2048]{0:T(1024)(128)(2,1)S(1)}, bf16[1024]{0:T(1024)(128)(2,1)S(1)}, bf16[4096]{0:T(1024)(128)(2,1)S(1)}, bf16[1024]{0:T(1024)(128)(2,1)S(1)}, bf16[6144]{0:T(1024)(128)(2,1)S(1)}) all-reduce(bf16[2048]{0:T(1024)(128)(2,1)S(1)} %pad_maximum_fusion.1, ...), channel_id=5, replica_groups=mesh['rep'=16,'shard'=8] {'shard'}, use_global_device_ids=true, to_apply=%region_24.0.clone | all-reduce | flops 14336 | bytes 57344
  1317.5 35.8 %all-reduce.5 = (bf16[256]{0:T(256)(128)(2,1)S(1)}, bf16[128]{0:T(256)(128)(2,1)S(1)}, bf16[512]{0:T(512)(128)(2,1)S(1)}, bf16[128]{0:T(256)(128)(2,1)S(1)}, bf16[768]{0:T(1024)(128)(2,1)S(1)}) all-reduce(bf16[256]{0:T(256)(128)(2,1)S(1)} %dynamic-slice.1, ...), channel_id=1, replica_groups=mesh['rep'=16,'shard'=8] {'rep'}, use_global_device_ids=true, to_apply=%region_25.0 | all-reduce | flops 1792 | bytes 7168 | tf_op jit(solution)/shard_map/psum | solution.py:274
  1356.1 12.7 fusion.50
  1368.8 15.5 %psum.77 = f32[1,1024]{1,0:T(1,128)S(1)} all-reduce(f32[1,1024]{1,0:T(1,128)S(1)} %fusion.50), channel_id=1, replica_groups=mesh['rep'=16,'shard'=8] {'shard'}, use_global_device_ids=true, to_apply=%region_19.0 | all-reduce | flops 1024 | bytes 8192 | tf_op jit(solution)/shard_map/psum | solution.py:229
  1384.9 32.3 %all-reduce.10.cloned.1.call-done = (bf16[128,3072]{1,0:T(8,128)(2,1)}, bf16[128,1024]{1,0:T(8,128)(2,1)}, bf16[128,4096]{1,0:T(8,128)(2,1)}, bf16[512,1024]{1,0:T(8,128)(2,1)}, bf16[128,6144]{1,0:T(8,128)(2,1)}) async-done(((bf16[128,3072]{1,0:T(8,128)(2,1)}, bf16[128,1024]{1,0:T(8,128)(2,1)}, bf16[128,4096]{1,0:T(8,128)(2,1)}, bf16[512,1024]{1,0:T(8,128)(2,1)}, bf16[128,6144]{1,0:T(8,128)(2,1)}), ...) | async-done | bytes 4718608 | tf_op jit(solution)/shard_map/psum | solution.py:273
  (168 shorter events, 115.3 us)
Async XLA Ops:
  7.2 151.0 %all-gather.13.cloned.1.call-start = ((), (), s32[]{:S(2)}) async-start(), calls=%async_computation.4 | async-start | bytes 14155776 | tf_op jit(solution)/shard_map/all_gather | solution.py:72
  7.9 239.3 %all-gather.15.cloned.1.call-start = ((), (), s32[]{:S(2)}) async-start(), calls=%async_computation.5 | async-start | bytes 7077888 | tf_op jit(solution)/shard_map/all_gather | solution.py:64
  8.7 295.4 %all-gather.17.cloned.1.call-start = ((), (), s32[]{:S(2)}) async-start(), calls=%async_computation.6 | async-start | bytes 2359296 | tf_op jit(solution)/shard_map/all_gather | solution.py:99
  60.6 186.7 %copy-start.3 = (bf16[1,128,1024]{2,1,0:T(8,128)(2,1)S(1)}, bf16[1,128,1024]{2,1,0:T(8,128)(2,1)}, u32[]{:S(2)}) copy-start(bf16[1,128,1024]{2,1,0:T(8,128)(2,1)} %param.13) | copy-start | bytes 786436
  251.1 3.7 copy-start.26
  252.0 106.7 %all-gather.19.cloned.1.call-start = ((), (), s32[]{:S(2)}) async-start(), calls=%async_computation.7 | async-start | bytes 2359296 | tf_op jit(solution)/shard_map/all_gather | solution.py:98
  252.8 159.9 %all-gather.21.cloned.1.call-start = ((), (), s32[]{:S(2)}) async-start(), calls=%async_computation.8 | async-start | bytes 2359296 | tf_op jit(solution)/shard_map/all_gather | solution.py:66
  253.4 266.4 %all-gather.23.cloned.1.call-start = ((), (), s32[]{:S(2)}) async-start(), calls=%async_computation.9 | async-start | bytes 9437184 | tf_op jit(solution)/shard_map/all_gather | solution.py:68
  254.0 373.1 %all-gather.25.cloned.1.call-start = ((), (), s32[]{:S(2)}) async-start(), calls=%async_computation.10 | async-start | bytes 9437184 | tf_op jit(solution)/shard_map/all_gather | solution.py:70
  254.7 482.8 %reduce-scatter.15.cloned.1.call-start = ((), (), s32[]{:S(2)}) async-start(), calls=%async_computation.14 | async-start | bytes 2359296
  295.5 66.0 %copy-start.10 = (bf16[1,128,1024]{1,2,0:T(8,128)(2,1)}, bf16[1,128,1024]{1,2,0:T(8,128)(2,1)S(1)}, u32[]{:S(2)}) copy-start(bf16[1,128,1024]{1,2,0:T(8,128)(2,1)S(1)} %copy.41) | copy-start | bytes 786436
  369.0 150.8 %copy-start.23 = (bf16[16,64,128]{2,1,0:T(8,128)(2,1)}, bf16[16,64,128]{2,1,0:T(8,128)(2,1)S(1)}, u32[]{:S(2)}) copy-start(bf16[16,64,128]{2,1,0:T(8,128)(2,1)S(1)} %fusion.16) | copy-start | bytes 786436
  519.8 107.3 %copy-start.16 = (bf16[1,128,1024]{2,1,0:T(8,128)(2,1)S(1)}, bf16[1,128,1024]{2,1,0:T(8,128)(2,1)}, u32[]{:S(2)}) copy-start(bf16[1,128,1024]{2,1,0:T(8,128)(2,1)} %param.15) | copy-start | bytes 786436
  627.1 8.3 copy-start.1
  635.4 4.1 copy-start.17
  635.4 5.0 copy-start.6
  665.6 149.9 %reduce-scatter.13.cloned.1.call-start = ((), (), s32[]{:S(2)}) async-start(), calls=%async_computation.13 | async-start | bytes 2359296
  672.7 6.7 copy-start.11
  692.4 4.5 copy-start.24
  692.4 4.5 copy-start.27
  696.9 469.2 %reduce-scatter.9.cloned.1.call-start = ((), (), s32[]{:S(2)}) async-start(), calls=%async_computation.11 | async-start | bytes 33030144 | tf_op jit(solution)/shard_map/reduce_scatter | solution.py:238
  719.0 3.9 copy-start.9
  722.9 94.8 %copy-start.20 = (bf16[16,64,128]{2,1,0:T(8,128)(2,1)}, bf16[16,64,128]{2,1,0:T(8,128)(2,1)S(1)}, u32[]{:S(2)}) copy-start(bf16[16,64,128]{2,1,0:T(8,128)(2,1)S(1)} %get-tuple-element.64) | copy-start | bytes 786436
  739.6 78.1 %copy-start.21 = (bf16[1,128,1024]{1,2,0:T(8,128)(2,1)}, bf16[1,128,1024]{1,2,0:T(8,128)(2,1)S(1)}, u32[]{:S(2)}) copy-start(bf16[1,128,1024]{1,2,0:T(8,128)(2,1)S(1)} %copy.48) | copy-start | bytes 786436
  822.9 8.7 copy-start.4
  822.9 8.7 copy-start.14
  837.9 7.5 copy-start.5
  864.4 419.0 %reduce-scatter.11.cloned.1.call-start = ((), (), s32[]{:S(2)}) async-start(), calls=%async_computation.12 | async-start | bytes 9437184 | tf_op jit(solution)/shard_map/reduce_scatter | solution.py:245
  871.0 546.3 %all-reduce.10.cloned.1.call-start = ((), (), s32[]{:S(2)}) async-start(), calls=%async_computation.15 | async-start | bytes 9437184 | tf_op jit(solution)/shard_map/psum | solution.py:273
  1172.1 111.3 %copy-start.28 = (u32[128]{0:T(128)S(1)}, u32[128]{0:T(128)}, u32[]{:S(2)}) copy-start(u32[128]{0:T(128)} %constant.43) | copy-start | bytes 1540
  1417.3 7.2 copy-start.19
  1419.1 6.9 copy-start.15
  (9 other events, 18.9 us)
Sparse Core Ops, SparseCore 0:
  10.3 147.8 all-gather.12
  160.5 86.6 all-gather.14
  252.1 51.9 all-gather.16
  306.9 51.7 all-gather.18
  360.9 51.7 all-gather.20
  414.9 104.8 all-gather.22
  522.2 104.8 all-gather.24
  665.8 71.7 reduce-scatter.14
  741.8 73.6 reduce-scatter.12
  864.5 301.5 reduce-scatter.8
  1169.9 113.4 reduce-scatter.10
  1287.5 129.6 all-reduce.9
where the time goes:
time: 1440 us
  waiting for transfers between devices  1010 us (70%)
  blocking collectives  185 us (13%)
  matrix products  99.4 us (7%)
  local copies, waits for them, and re-layouts  64.5 us (4%)
  other arithmetic  55.1 us (4%)
  between operations  17.5 us (1%)
    reduce_scatter x1, waiting for transfers between devices, on_device(): lax.psum_scatter(jnp.concatenate(pieces, axis=1).astype(jnp.bfloat16), 's...  295 us
    reduce_scatter x1, waiting for transfers between devices, on_device(): lax.psum_scatter(jnp.einsum('lrc,lre->ce', active_low, grad_branch_second...  109 us
    all_gather x1, waiting for transfers between devices, on_device(): lax.all_gather(w_fc1, 'shard', axis=0, tiled=True)  104 us
    all_gather x1, waiting for transfers between devices, on_device(): lax.all_gather(w_fc2, 'shard', axis=0, tiled=True)  101 us
    all_gather x1, waiting for transfers between devices, on_device(): lax.all_gather(w_ada, 'shard', axis=0, tiled=True)  97.7 us
    unnamed x14, waiting for transfers between devices  88.2 us
    all_gather x1, waiting for transfers between devices, on_device(): lax.all_gather(w_qkv, 'shard', axis=0, tiled=True)  82.7 us
    all_gather x1, waiting for transfers between devices, on_device(): lax.all_gather(keyset, 'shard', axis=1, tiled=True)  50.7 us
  transfers between devices with their start and end apart: 12, of which 12 were waited for; matrix products, arithmetic and copies ran while one was open for 8% of the time, Pallas kernels for 0%

commit v1 on v0

v1 whole, which is shorter than its diff:
```python
import jax
import jax.numpy as jnp
from jax import lax
from jax.sharding import Mesh, PartitionSpec as P

HEAD = 64
SHARD = ("xh", "y")
CHIPS = ("xl", "z")
REP = ("xl", "z", "core")
OFFSETS = ((0, 0), (0, 1), (0, 3), (0, 2), (1, 0), (1, 1), (1, 3), (1, 2))

epsilon = 1e-06
highest = lax.Precision.HIGHEST
low = jnp.bfloat16
wide = jnp.float32


def shift(value, dx, dy):
    pairs = [(x * 4 + y, ((x + dx) % 2) * 4 + (y + dy) % 4) for x in range(2) for y in range(4)]
    return lax.ppermute(value, SHARD, pairs)


def gather_turned(value):
    return [value] + [shift(value, dx, dy) for dx, dy in OFFSETS[1:]]


def scatter_turned(parts):
    total = parts[0]
    for part, (dx, dy) in zip(parts[1:], OFFSETS[1:]):
        total = total + shift(part.astype(low), dx, (4 - dy) % 4).astype(wide)
    return total


def swap_core(value):
    return lax.ppermute(value, "core", [(0, 1), (1, 0)])


def exchange(value, axes=SHARD):
    return lax.all_to_all(value, axes, 0, 0, tiled=True)


def spread(value, axes=SHARD, count=8):
    return exchange(jnp.broadcast_to(value[None], (count,) + value.shape), axes)


def normalize(values):
    centered = values - jnp.mean(values, axis=-1, keepdims=True)
    inverse = lax.rsqrt(jnp.mean(centered * centered, axis=-1, keepdims=True) + epsilon)
    return centered * inverse, inverse


def normalize_back(norm, inverse, grad):
    return inverse * (
        grad
        - jnp.mean(grad, axis=-1, keepdims=True)
        - norm * jnp.mean(grad * norm, axis=-1, keepdims=True)
    )


def silu(values):
    return values / (1.0 + jnp.exp(-values))


def gelu_tanh(values):
    return (
        0.5
        * values
        * (1.0 + jnp.tanh(0.7978845608028654 * (values + 0.044715 * values * values * values)))
    )


def mul(left, right):
    return lax.dot_general(left, right, (((1,), (0,)), ((), ())), preferred_element_type=wide)


def mul_t(left, right):
    return lax.dot_general(left, right, (((1,), (1,)), ((), ())), preferred_element_type=wide)


def t_mul(left, right):
    return lax.dot_general(left, right, (((0,), (0,)), ((), ())), preferred_element_type=wide)


def core_half(value, core):
    half = value.shape[0] // 2
    keep = lax.dynamic_slice_in_dim(value, core * half, half, 0)
    give = lax.dynamic_slice_in_dim(value, (1 - core) * half, half, 0).astype(low)
    return keep + swap_core(give).astype(wide)


def core_join(value, core):
    other = swap_core(value)
    first = jnp.where(core == 0, value, other)
    second = jnp.where(core == 0, other, value)
    return jnp.concatenate([first, second], axis=0)


def on_device(
    latents, cond, cotangent, w_qkv, bias_qv, w_proj, b_proj, w_fc1, b_fc1, w_fc2, b_fc2, w_ada, b_ada
):
    stream_low = latents[0]
    upstream_low = cotangent[0]
    rows, features = stream_low.shape
    shards = 8
    own = features // shards
    units = w_fc2.shape[0]
    heads = own // HEAD
    place = lax.axis_index(SHARD)
    core = lax.axis_index("core")
    score_scale = HEAD ** (-0.5)

    cond_value = cond.astype(wide)
    cond_silu, silu_pull = jax.vjp(silu, cond_value)
    cond_low = cond_silu.astype(low)
    cond_own = lax.dynamic_slice_in_dim(cond_low, place * own, own, 1)
    mod_part = mul(cond_own, w_ada)[0]
    ada_width = w_ada.shape[1]
    blocks = jnp.arange(shards)[:, None] == place
    mod_part = mod_part + jnp.where(blocks, b_ada.astype(wide)[None, :], 0.0).reshape(ada_width)
    small = jnp.concatenate(
        [mod_part, bias_qv.astype(wide), b_proj.astype(wide), b_fc2.astype(wide)]
    )
    small_all = spread(small)
    modulation = jnp.sum(small_all[:, :ada_width], axis=0)
    shift_first, scale_first, gate_first, shift_second, scale_second, gate_second = jnp.split(
        modulation[None, :], 6, axis=1
    )
    at = ada_width
    bias_wide = small_all[:, at : at + 2 * own].reshape(1, 2 * features)
    at += 2 * own
    proj_bias = small_all[:, at : at + own].reshape(1, features)
    at += own
    second_bias = small_all[:, at : at + own].reshape(1, features)

    tokens = spread(stream_low).reshape(shards * rows, features)
    wq = exchange(
        w_qkv.reshape(own, 3, shards, own).transpose(2, 0, 1, 3).reshape(shards, own, 3 * own)
    ).reshape(features, 3 * own)
    w1 = exchange(w_fc1.reshape(own, shards, units).transpose(1, 0, 2)).reshape(features, units)
    wp = spread(w_proj).reshape(features, features)
    upstream_all = jnp.concatenate(gather_turned(upstream_low), axis=0)

    norm_first, inverse_first = normalize(tokens.astype(wide))
    attend_in = (norm_first * (1.0 + scale_first) + shift_first).astype(low)
    packed = mul(attend_in, wq)
    query_bias = lax.dynamic_slice_in_dim(bias_wide, place * own, own, 1)
    value_bias = lax.dynamic_slice_in_dim(bias_wide, features + place * own, own, 1)
    queries = (packed[:, :own] + query_bias).astype(low)
    keyset = packed[:, own : 2 * own].astype(low)
    valueset = (packed[:, 2 * own :] + value_bias).astype(low)
    length = shards * rows

    def split(value):
        return value.reshape(length, heads, HEAD)

    query_heads, key_heads, value_heads = split(queries), split(keyset), split(valueset)
    scores = (
        jnp.einsum("qhe,khe->hqk", query_heads, key_heads, preferred_element_type=wide)
        * score_scale
    )
    row_peak = jnp.max(scores, axis=-1, keepdims=True)
    powered = jnp.exp(scores - row_peak)
    row_total = jnp.sum(powered, axis=-1, keepdims=True)
    attention = powered / row_total
    log_total = row_peak + jnp.log(row_total)
    mixed = (
        jnp.einsum("hqk,khe->qhe", attention.astype(low), value_heads, preferred_element_type=wide)
        .reshape(length, own)
        .astype(low)
    )
    mixed_tok = exchange(mixed.reshape(shards, rows, own))
    mixed_tok = mixed_tok.transpose(1, 0, 2).reshape(rows, features)
    branch = mul(mixed_tok, wp) + proj_bias
    stream = stream_low.astype(wide)
    middle = stream + gate_first * branch
    norm_second, inverse_second = normalize(middle)
    feed_in = (norm_second * (1.0 + scale_second) + shift_second).astype(low)
    feed_all = jnp.concatenate(gather_turned(feed_in), axis=0)
    hidden = mul(feed_all, w1) + b_fc1.astype(wide)[None, :]
    active_value, gelu_pull = jax.vjp(gelu_tanh, hidden)
    active = active_value.astype(low)
    branch_second_part = mul(active, w_fc2)

    def turned_parts(value):
        return [value[k * rows : (k + 1) * rows] for k in range(shards)]

    grad_branch_second = (upstream_all.astype(wide) * gate_second).astype(low)
    grad_active = mul_t(grad_branch_second, w_fc2)
    grad_hidden = gelu_pull(grad_active)[0].astype(low)
    grad_feed = scatter_turned(turned_parts(mul_t(grad_hidden, w1)))

    branch_second = scatter_turned(turned_parts(branch_second_part)) + second_bias
    output = (middle + gate_second * branch_second).astype(low)

    upstream = upstream_low.astype(wide)
    grad_gate_second = jnp.sum(upstream * branch_second, axis=0)
    grad_scale_second = jnp.sum(grad_feed * norm_second, axis=0)
    grad_shift_second = jnp.sum(grad_feed, axis=0)
    grad_middle = upstream + normalize_back(
        norm_second, inverse_second, grad_feed * (1.0 + scale_second)
    )
    grad_gate_first = jnp.sum(grad_middle * branch, axis=0)
    grad_branch = (grad_middle * gate_first).astype(low)
    grad_mixed_tok = mul_t(grad_branch, wp).astype(low)
    grad_mixed = exchange(grad_mixed_tok.reshape(rows, shards, own).transpose(1, 0, 2))
    grad_mixed = split(grad_mixed.reshape(length, own))

    again_scores = (
        jnp.einsum("qhe,khe->hqk", query_heads, key_heads, preferred_element_type=wide)
        * score_scale
    )
    again = jnp.exp(again_scores - log_total)
    grad_probs = jnp.einsum("qhe,khe->hqk", grad_mixed, value_heads, preferred_element_type=wide)
    grad_value = jnp.einsum(
        "hqk,qhe->khe", again.astype(low), grad_mixed, preferred_element_type=wide
    )
    row_delta = jnp.sum(again * grad_probs, axis=-1, keepdims=True)
    grad_scores = (again * (grad_probs - row_delta)).astype(low)
    grad_query = (
        jnp.einsum("hqk,khe->qhe", grad_scores, key_heads, preferred_element_type=wide)
        * score_scale
    )
    grad_key = (
        jnp.einsum("hqk,qhe->khe", grad_scores, query_heads, preferred_element_type=wide)
        * score_scale
    )
    grad_packed = jnp.concatenate(
        [part.reshape(length, own).astype(low) for part in (grad_query, grad_key, grad_value)],
        axis=1,
    )
    attend_part = mul_t(grad_packed, wq)
    grad_scale_first = jnp.sum(attend_part * norm_first, axis=0)
    grad_shift_first = jnp.sum(attend_part, axis=0)
    attend_sent = exchange(attend_part.astype(low).reshape(shards, rows, features))
    grad_attend = jnp.sum(attend_sent.astype(wide), axis=0)
    norm_own, inverse_own = normalize(stream)
    grad_stream = grad_middle + normalize_back(
        norm_own, inverse_own, grad_attend * (1.0 + scale_first)
    )
    grad_latents = grad_stream.astype(low)

    mod_terms = jnp.concatenate(
        [
            grad_shift_first,
            grad_scale_first,
            grad_gate_first,
            grad_shift_second,
            grad_scale_second,
            grad_gate_second,
            jnp.sum(grad_branch.astype(wide), axis=0),
        ]
    )
    mod_sums = jnp.sum(spread(mod_terms), axis=0)
    grad_modulation = mod_sums[:ada_width]
    proj_bias_term = lax.dynamic_slice_in_dim(mod_sums, ada_width + place * own, own, 0)
    cond_term = jnp.sum(w_ada.astype(wide) * grad_modulation[None, :], axis=1)
    cond_total = spread(cond_term).reshape(1, features)
    grad_cond = silu_pull(cond_total)[0]

    packed_sums = jnp.sum(grad_packed.astype(wide), axis=0)
    second_bias_sums = jnp.sum(grad_branch_second.astype(wide), axis=0)
    rep_terms = jnp.concatenate(
        [
            grad_modulation,
            cond_own[0].astype(wide),
            proj_bias_term,
            jnp.sum(grad_hidden.astype(wide), axis=0),
            lax.dynamic_slice_in_dim(second_bias_sums, place * own, own, 0),
            packed_sums,
        ]
    )
    rep_all = spread(rep_terms, REP, 16)
    grad_w_ada = lax.dot_general(
        rep_all[:, ada_width : ada_width + own],
        rep_all[:, :ada_width],
        (((0,), (0,)), ((), ())),
        precision=highest,
        preferred_element_type=wide,
    )
    rep_sums = jnp.sum(rep_all, axis=0)
    ada_own = ada_width // shards
    grad_b_ada = lax.dynamic_slice_in_dim(rep_sums, place * ada_own, ada_own, 0)
    at = ada_width + own
    grad_b_proj = rep_sums[at : at + own]
    at += own
    grad_b_fc1 = rep_sums[at : at + units]
    at += units
    grad_b_fc2 = rep_sums[at : at + own]
    at += own
    bias_all = spread(jnp.concatenate([rep_sums[at : at + own], rep_sums[at + 2 * own :]]))
    bias_all = jnp.concatenate(
        [bias_all[:, :own].reshape(features), bias_all[:, own:].reshape(features)]
    )
    grad_bias_qv = lax.dynamic_slice_in_dim(bias_all, place * 2 * own, 2 * own, 0)

    def over_rep(value):
        owned = lax.psum_scatter(value.astype(low), CHIPS, scatter_dimension=0, tiled=True)
        return core_join(lax.all_gather(owned, CHIPS, axis=0, tiled=True), core).astype(wide)

    term_second = core_half(t_mul(active, grad_branch_second), core)
    grad_w_fc2 = over_rep(term_second)

    term_first = core_half(t_mul(feed_all, grad_hidden).reshape(shards, own, units).transpose(1, 0, 2).reshape(own, shards * units), core)
    term_first = exchange(
        term_first.astype(low).reshape(own // 2, shards, units).transpose(1, 0, 2)
    )
    term_first = term_first.transpose(1, 0, 2).reshape(own // 2, shards * units)
    grad_w_fc1 = over_rep(term_first)

    term_proj = t_mul(mixed_tok, grad_branch).reshape(shards, own, features)
    term_proj = core_half(term_proj.transpose(1, 0, 2), core)
    term_proj = exchange(term_proj.astype(low).transpose(1, 0, 2))
    grad_w_proj = over_rep(jnp.sum(term_proj.astype(wide), axis=0))

    term_qkv = t_mul(attend_in, grad_packed).reshape(shards, own, 3 * own)
    term_qkv = core_half(term_qkv.transpose(1, 0, 2), core)
    term_qkv = exchange(term_qkv.astype(low).transpose(1, 0, 2))
    term_qkv = (
        term_qkv.reshape(shards, own // 2, 3, own)
        .transpose(1, 2, 0, 3)
        .reshape(own // 2, 3 * features)
    )
    grad_w_qkv = over_rep(term_qkv)

    return (
        output[None],
        grad_latents[None],
        grad_cond,
        grad_w_qkv,
        grad_bias_qv,
        grad_w_proj,
        grad_b_proj,
        grad_w_fc1,
        grad_b_fc1,
        grad_w_fc2,
        grad_b_fc2,
        grad_w_ada,
        grad_b_ada,
    )


def solution(mesh):
    fine = Mesh(mesh.devices.reshape(2, 4, 2, 2, 4), REP + SHARD)
    tokens = P(REP, SHARD, None)
    matrix = P(SHARD, None)
    vector = P(SHARD)
    params = (matrix, vector) * 5
    return jax.shard_map(
        on_device,
        mesh=fine,
        in_specs=(tokens, P(REP, None), tokens) + params,
        out_specs=(tokens, tokens, P(REP, None)) + params,
        check_vma=False,
    )
```

time: 1440 us -> 628 us (0.44)
  waiting for transfers between devices: 1010 us -> 123 us
  starting transfers between devices: 0.69 us -> 185 us
  blocking collectives: 185 us -> 118 us
  matrix products: 99.4 us -> 57 us
    all_gather x7 -> x0, waiting for transfers between devices: 488 us -> none  [the longest x1 104 us: on_device(): lax.all_gather(w_fc1, 'shard', axis=0, tiled=True)]
    reduce_scatter x2 -> x4, waiting for transfers between devices: 404 us -> 18.5 us  [over_rep(): lax.psum_scatter(value.astype(low), CHIPS, scatter_dimension=0, tiled=True)]
    ppermute x0 -> x36, starting transfers between devices: none -> 104 us  [the longest x28 63.8 us: shift(): return lax.ppermute(value, SHARD, pairs)]
    unnamed x14 -> x4, waiting for transfers between devices: 88.2 us -> 0.07 us
    all_to_all x0 -> x15, starting transfers between devices: none -> 81 us  [exchange(): return lax.all_to_all(value, axes, 0, 0, tiled=True)]
    all_to_all x0 -> x15, waiting for transfers between devices: none -> 69.1 us  [exchange(): return lax.all_to_all(value, axes, 0, 0, tiled=True)]
    psum x2 -> x0, blocking collectives: 51.3 us -> none  [the longest x1 35.8 us: on_device(): lax.psum(bias_owned[0].astype(jnp.bfloat16), 'rep').astype(jnp.float32)]
    dot_general x20, matrix products: 99.4 us -> 57 us  [the longest x4 15.7 us: mul_t(): lax.dot_general(left, right, (((1,), (1,)), ((), ())), preferred_element_...]
  transfers between devices with their start and end apart: 12 -> 55, of which waited for: 12 -> 23; matrix products, arithmetic and copies ran while one was open for 8% -> 22% of each run, Pallas kernels for 0% -> 0%
where the time goes in v1:
time: 628 us; the launch traced here: 620 us
  starting transfers between devices  185 us (29%)
  waiting for transfers between devices  123 us (20%)
  blocking collectives  118 us (19%)
  local copies, waits for them, and re-layouts  78.6 us (13%)
  matrix products  57 us (9%)
  other arithmetic  43 us (7%)
  between operations  14.9 us (2%)
    all_gather x4, blocking collectives, over_rep(): lax.all_gather(owned, CHIPS, axis=0, tiled=True)  118 us
    all_to_all x15, starting transfers between devices, exchange(): return lax.all_to_all(value, axes, 0, 0, tiled=True)  81 us
    all_to_all x15, waiting for transfers between devices, exchange(): return lax.all_to_all(value, axes, 0, 0, tiled=True)  69.1 us
    ppermute x28, starting transfers between devices, shift(): return lax.ppermute(value, SHARD, pairs)  63.8 us
    ppermute x8, starting transfers between devices, swap_core(): return lax.ppermute(value, 'core', [(0, 1), (1, 0)])  40 us
    ppermute x28, waiting for transfers between devices, shift(): return lax.ppermute(value, SHARD, pairs)  35.6 us
    unnamed x123, local copies, waits for them, and re-layouts  33.5 us
    reduce_scatter x4, waiting for transfers between devices, over_rep(): lax.psum_scatter(value.astype(low), CHIPS, scatter_dimension=0, tiled=True)  18.5 us
  transfers between devices with their start and end apart: 55, of which 23 were waited for; matrix products, arithmetic and copies ran while one was open for 22% of the time, Pallas kernels for 0%

profile of v1, /device:TPU:1, one launch (start us, length us, event | category | flops | bytes accessed | tf_op | source)
XLA Modules:
  0.0 620.4 jit_solution(15007044505543565158)
XLA Ops:
  14.0 7.5 %all-to-all-start = ((f32[8,1,6656]{2,1,0:T(1,128)}), f32[8,1,6656]{2,1,0:T(1,128)S(1)}, u32[]{:S(2)}, u32[]{:S(2)}) async-start(f32[8,1,6656]{2,1,0:T(1,128)} %broadcast_in_dim.43), calls=%async_computation | async-start | bytes 425984 | tf_op jit(solution)/shard_map/all_to_all | solution.py:39
  24.0 4.8 all-to-all-done
  32.4 5.0 collective-permute-start.19
  44.0 8.9 %all-to-all-start.1 = ((bf16[8,128,1024]{2,1,0:T(8,128)(2,1)}), bf16[8,128,1024]{2,1,0:T(8,128)(2,1)S(1)}, u32[]{:S(2)}, u32[]{:S(2)}) async-start(bf16[8,128,1024]{2,1,0:T(8,128)(2,1)} %broadcast_in_dim.45), calls=%async_computation.1 | async-start | bytes 4194304 | tf_op jit(solution)/shard_map/all_to_all | solution.py:39
  55.6 6.9 %collective-permute-done.14 = bf16[128,1024]{1,0:T(8,128)(2,1)} collective-permute-done((bf16[128,1024]{1,0:T(8,128)(2,1)}, bf16[128,1024]{1,0:T(8,128)(2,1)}, u32[]{:S(2)}, u32[]{:S(2)}) %collective-permute-start.14) | collective-permute-done | bytes 262176 | tf_op jit(solution)/shard_map/ppermute | solution.py:20
  62.5 7.4 %collective-permute-start.17 = (bf16[128,1024]{1,0:T(8,128)(2,1)}, bf16[128,1024]{1,0:T(8,128)(2,1)S(1)}, u32[]{:S(2)}, u32[]{:S(2)}) collective-permute-start(bf16[128,1024]{1,0:T(8,128)(2,1)} %bitcast.30), channel_id=1, source_target_pairs={{0,4},{1,5},{2,6},{3,7},{4,0},{5,1},{6,2},{7,3},{8,12},{9,13},{10,... | collective-permute-start | bytes 786440 | tf_op jit(solution)/shard_map/ppermute | solution.py:20
  82.1 5.0 all-to-all-done.1
  106.7 9.4 %all-to-all-done.4 = bf16[8,128,1024]{2,1,0:T(8,128)(2,1)} async-done(((bf16[8,128,1024]{2,1,0:T(8,128)(2,1)}), bf16[8,128,1024]{2,1,0:T(8,128)(2,1)}, u32[]{:S(2)}, u32[]{:S(2)}) %all-to-all-start.4) | async-done | bytes 2097184 | tf_op jit(solution)/shard_map/all_to_all | solution.py:39
  116.1 9.3 %all-to-all-start.3 = ((bf16[8,128,128]{2,1,0:T(8,128)(2,1)}), bf16[8,128,128]{2,1,0:T(8,128)(2,1)}, u32[]{:S(2)}, u32[]{:S(2)}) async-start(bf16[8,128,128]{2,1,0:T(8,128)(2,1)} %copy.166), calls=%async_computation.3 | async-start | bytes 524288 | tf_op jit(solution)/shard_map/all_to_all | solution.py:39
  145.1 5.3 all-to-all-done.5
  168.0 9.5 %collective-permute-done.1 = bf16[128,1024]{1,0:T(8,128)(2,1)} collective-permute-done((bf16[128,1024]{1,0:T(8,128)(2,1)}, bf16[128,1024]{1,0:T(8,128)(2,1)}, u32[]{:S(2)}, u32[]{:S(2)}) %collective-permute-start.1) | collective-permute-done | bytes 262176 | tf_op jit(solution)/shard_map/ppermute | solution.py:20
  177.5 7.0 %collective-permute-start.4 = (bf16[128,1024]{1,0:T(8,128)(2,1)}, bf16[128,1024]{1,0:T(8,128)(2,1)S(1)}, u32[]{:S(2)}, u32[]{:S(2)}) collective-permute-start(bf16[128,1024]{1,0:T(8,128)(2,1)} %get-tuple-element.28), channel_id=1, source_target_pairs={{0,5},{1,6},{2,7},{3,4},{4,1},{5,2},{6,3},{7,0},{8,13},{9,14},{10,... | collective-permute-start | bytes 786440 | tf_op jit(solution)/shard_map/ppermute | solution.py:20
  235.7 5.9 collective-permute-start.25
  241.6 5.0 collective-permute-done.21
  298.1 5.1 fusion.16
  338.9 9.3 %all-to-all-done.14 = bf16[8,64,512]{2,1,0:T(8,128)(2,1)S(1)} async-done(((bf16[8,64,512]{2,1,0:T(8,128)(2,1)}), bf16[8,64,512]{2,1,0:T(8,128)(2,1)S(1)}, u32[]{:S(2)}, u32[]{:S(2)}) %all-to-all-start.14) | async-done | bytes 524320 | tf_op jit(solution)/shard_map/all_to_all | solution.py:39
  355.2 4.9 all-to-all-done.10
  365.1 10.5 %all-to-all-done.13 = bf16[8,64,1024]{2,1,0:T(8,128)(2,1)S(1)} async-done(((bf16[8,64,1024]{2,1,0:T(8,128)(2,1)}), bf16[8,64,1024]{2,1,0:T(8,128)(2,1)S(1)}, u32[]{:S(2)}, u32[]{:S(2)}) %all-to-all-start.13) | async-done | bytes 1048608 | tf_op jit(solution)/shard_map/all_to_all | solution.py:39
  375.7 7.3 %all-to-all-start.7 = ((bf16[8,128,1024]{2,1,0:T(8,128)(2,1)}), bf16[8,128,1024]{2,1,0:T(8,128)(2,1)S(1)}, u32[]{:S(2)}, u32[]{:S(2)}) async-start(bf16[8,128,1024]{2,1,0:T(8,128)(2,1)} %bitcast.216), calls=%async_computation.7 | async-start | bytes 4194304 | tf_op jit(solution)/shard_map/all_to_all | solution.py:39
  387.3 46.3 %all_gather.15 = bf16[256,1024]{1,0:T(8,128)(2,1)} all-gather(bf16[32,1024]{1,0:T(8,128)(2,1)} %reduce-scatter.11.cloned.1.call-done), channel_id=1, replica_groups=mesh['xl'=2,'z'=4,'core'=2,'xh'=2,'y'=4] {'xl','z'}, dimensions={0}, use_global_device_ids=true | all-gather | bytes 589824 | tf_op jit(solution)/shard_map/all_gather | solution.py:298
  433.7 6.3 %collective-permute-start.35 = (bf16[256,1024]{1,0:T(8,128)(2,1)}, bf16[256,1024]{1,0:T(8,128)(2,1)}, u32[]{:S(2)}, u32[]{:S(2)}) collective-permute-start(bf16[256,1024]{1,0:T(8,128)(2,1)} %all_gather.15), channel_id=1, source_target_pairs={{0,8},{8,0},{1,9},{9,1},{2,10},{10,2},{3,11},{11,3},{4,12},{12,4},... | collective-permute-start | bytes 1572872 | tf_op jit(solution)/shard_map/ppermute | solution.py:35
  441.3 24.8 %all_gather.12 = bf16[64,3072]{1,0:T(8,128)(2,1)} all-gather(bf16[8,3072]{1,0:T(8,128)(2,1)} %reduce-scatter.5.cloned.1.call-done), channel_id=1, replica_groups=mesh['xl'=2,'z'=4,'core'=2,'xh'=2,'y'=4] {'xl','z'}, dimensions={0}, use_global_device_ids=true | all-gather | bytes 442368 | tf_op jit(solution)/shard_map/all_gather | solution.py:298
  466.2 6.1 collective-permute-start.29
  472.3 25.2 %all_gather.14 = bf16[64,4096]{1,0:T(8,128)(2,1)} all-gather(bf16[8,4096]{1,0:T(8,128)(2,1)} %reduce-scatter.9.cloned.1.call-done), channel_id=1, replica_groups=mesh['xl'=2,'z'=4,'core'=2,'xh'=2,'y'=4] {'xl','z'}, dimensions={0}, use_global_device_ids=true | all-gather | bytes 589824 | tf_op jit(solution)/shard_map/all_gather | solution.py:298
  497.5 6.0 collective-permute-start.33
  510.3 7.3 %all-to-all-start.8 = ((f32[8,1,7168]{2,1,0:T(1,128)}), f32[8,1,7168]{2,1,0:T(1,128)S(1)}, u32[]{:S(2)}, u32[]{:S(2)}) async-start(f32[8,1,7168]{2,1,0:T(1,128)} %broadcast_in_dim.49), calls=%async_computation.8 | async-start | bytes 458752 | tf_op jit(solution)/shard_map/all_to_all | solution.py:39
  520.2 18.4 %reduce-scatter.7.cloned.1.call-done = bf16[8,1024]{1,0:T(8,128)(2,1)} async-done(((bf16[64,1024]{1,0:T(8,128)(2,1)}), bf16[8,1024]{1,0:T(8,128)(2,1)}) %reduce-scatter.7.cloned.1.call-update) | async-done | bytes 16400 | tf_op jit(solution)/shard_map/reduce_scatter | solution.py:297
  538.7 22.0 %all_gather.13 = bf16[64,1024]{1,0:T(8,128)(2,1)S(1)} all-gather(bf16[8,1024]{1,0:T(8,128)(2,1)} %reduce-scatter.7.cloned.1.call-done), channel_id=1, replica_groups=mesh['xl'=2,'z'=4,'core'=2,'xh'=2,'y'=4] {'xl','z'}, dimensions={0}, use_global_device_ids=true | all-gather | bytes 147456 | tf_op jit(solution)/shard_map/all_gather | solution.py:298
  560.7 12.2 %collective-permute-start.31 = (bf16[64,1024]{1,0:T(8,128)(2,1)S(1)}, bf16[64,1024]{1,0:T(8,128)(2,1)S(1)}, u32[]{:S(2)}, u32[]{:S(2)}) collective-permute-start(bf16[64,1024]{1,0:T(8,128)(2,1)S(1)} %all_gather.13), channel_id=1, source_target_pairs={{0,8},{8,0},{1,9},{9,1},{2,10},{10,2},{3,11},{11,3},{4,12},{12,4},... | collective-permute-start | bytes 393224 | tf_op jit(solution)/shard_map/ppermute | solution.py:35
  574.1 6.1 all-to-all-start.9
  580.4 6.3 %all-to-all-done.9 = f32[8,1,128]{2,1,0:T(1,128)S(1)} async-done(((f32[8,1,128]{2,1,0:T(1,128)}), f32[8,1,128]{2,1,0:T(1,128)S(1)}, u32[]{:S(2)}, u32[]{:S(2)}) %all-to-all-start.9) | async-done | bytes 4128 | tf_op jit(solution)/shard_map/all_to_all | solution.py:39
  596.8 5.0 all-to-all-done.11
  (333 shorter events, 279.2 us)
Async XLA Ops:
  32.4 94.7 %collective-permute-start.19 = (bf16[128,1024]{1,0:T(8,128)(2,1)}, bf16[128,1024]{1,0:T(8,128)(2,1)}, u32[]{:S(2)}, u32[]{:S(2)}) collective-permute-start(bf16[128,1024]{1,0:T(8,128)(2,1)} %bitcast.30), channel_id=1, source_target_pairs={{0,7},{1,4},{2,5},{3,6},{4,3},{5,0},{6,1},{7,2},{8,15},{9,12},{10,... | collective-permute-start | bytes 786440 | tf_op jit(solution)/shard_map/ppermute | solution.py:20
  37.4 88.0 %collective-permute-start.18 = (bf16[128,1024]{1,0:T(8,128)(2,1)}, bf16[128,1024]{1,0:T(8,128)(2,1)}, u32[]{:S(2)}, u32[]{:S(2)}) collective-permute-start(bf16[128,1024]{1,0:T(8,128)(2,1)} %bitcast.30), channel_id=1, source_target_pairs={{0,5},{1,6},{2,7},{3,4},{4,1},{5,2},{6,3},{7,0},{8,13},{9,14},{10,... | collective-permute-start | bytes 786440 | tf_op jit(solution)/shard_map/ppermute | solution.py:20
  37.4 38.2 %collective-permute-start.16 = (bf16[128,1024]{1,0:T(8,128)(2,1)}, bf16[128,1024]{1,0:T(8,128)(2,1)}, u32[]{:S(2)}, u32[]{:S(2)}) collective-permute-start(bf16[128,1024]{1,0:T(8,128)(2,1)} %bitcast.30), channel_id=1, source_target_pairs={{0,2},{1,3},{2,0},{3,1},{4,6},{5,7},{6,4},{7,5},{8,10},{9,11},{10,... | collective-permute-start | bytes 786440 | tf_op jit(solution)/shard_map/ppermute | solution.py:20
  39.1 32.4 %collective-permute-start.15 = (bf16[128,1024]{1,0:T(8,128)(2,1)}, bf16[128,1024]{1,0:T(8,128)(2,1)}, u32[]{:S(2)}, u32[]{:S(2)}) collective-permute-start(bf16[128,1024]{1,0:T(8,128)(2,1)} %bitcast.30), channel_id=1, source_target_pairs={{0,3},{1,0},{2,1},{3,2},{4,7},{5,4},{6,5},{7,6},{8,11},{9,8},{10,9... | collective-permute-start | bytes 786440 | tf_op jit(solution)/shard_map/ppermute | solution.py:20
  40.1 22.4 %collective-permute-start.14 = (bf16[128,1024]{1,0:T(8,128)(2,1)}, bf16[128,1024]{1,0:T(8,128)(2,1)}, u32[]{:S(2)}, u32[]{:S(2)}) collective-permute-start(bf16[128,1024]{1,0:T(8,128)(2,1)} %bitcast.30), channel_id=1, source_target_pairs={{0,1},{1,2},{2,3},{3,0},{4,5},{5,6},{6,7},{7,4},{8,9},{9,10},{10,1... | collective-permute-start | bytes 786440 | tf_op jit(solution)/shard_map/ppermute | solution.py:20
  44.0 43.2 %all-to-all-start.1 = ((bf16[8,128,1024]{2,1,0:T(8,128)(2,1)}), bf16[8,128,1024]{2,1,0:T(8,128)(2,1)S(1)}, u32[]{:S(2)}, u32[]{:S(2)}) async-start(bf16[8,128,1024]{2,1,0:T(8,128)(2,1)} %broadcast_in_dim.45), calls=%async_computation.1 | async-start | bytes 4194304 | tf_op jit(solution)/shard_map/all_to_all | solution.py:39
  71.6 71.8 %collective-permute-start.20 = (bf16[128,1024]{1,0:T(8,128)(2,1)}, bf16[128,1024]{1,0:T(8,128)(2,1)}, u32[]{:S(2)}, u32[]{:S(2)}) collective-permute-start(bf16[128,1024]{1,0:T(8,128)(2,1)} %bitcast.30), channel_id=1, source_target_pairs={{0,6},{1,7},{2,4},{3,5},{4,2},{5,3},{6,0},{7,1},{8,14},{9,15},{10,... | collective-permute-start | bytes 786440 | tf_op jit(solution)/shard_map/ppermute | solution.py:20
  89.7 26.4 %all-to-all-start.4 = ((bf16[8,128,1024]{2,1,0:T(8,128)(2,1)}), bf16[8,128,1024]{2,1,0:T(8,128)(2,1)}, u32[]{:S(2)}, u32[]{:S(2)}) async-start(bf16[8,128,1024]{2,1,0:T(8,128)(2,1)} %broadcast_in_dim.46), calls=%async_computation.4 | async-start | bytes 4194304 | tf_op jit(solution)/shard_map/all_to_all | solution.py:39
  142.1 21.4 %collective-permute-start = (bf16[128,1024]{1,0:T(8,128)(2,1)}, bf16[128,1024]{1,0:T(8,128)(2,1)}, u32[]{:S(2)}, u32[]{:S(2)}) collective-permute-start(bf16[128,1024]{1,0:T(8,128)(2,1)} %get-tuple-element.28), channel_id=1, source_target_pairs={{0,1},{1,2},{2,3},{3,0},{4,5},{5,6},{6,7},{7,4},{8,9},{9,10},{10,1... | collective-permute-start | bytes 786440 | tf_op jit(solution)/shard_map/ppermute | solution.py:20
  152.7 33.5 %collective-permute-start.2 = (bf16[128,1024]{1,0:T(8,128)(2,1)}, bf16[128,1024]{1,0:T(8,128)(2,1)}, u32[]{:S(2)}, u32[]{:S(2)}) collective-permute-start(bf16[128,1024]{1,0:T(8,128)(2,1)} %get-tuple-element.28), channel_id=1, source_target_pairs={{0,2},{1,3},{2,0},{3,1},{4,6},{5,7},{6,4},{7,5},{8,10},{9,11},{10,... | collective-permute-start | bytes 786440 | tf_op jit(solution)/shard_map/ppermute | solution.py:20
  155.4 22.1 %collective-permute-start.1 = (bf16[128,1024]{1,0:T(8,128)(2,1)}, bf16[128,1024]{1,0:T(8,128)(2,1)}, u32[]{:S(2)}, u32[]{:S(2)}) collective-permute-start(bf16[128,1024]{1,0:T(8,128)(2,1)} %get-tuple-element.28), channel_id=1, source_target_pairs={{0,3},{1,0},{2,1},{3,2},{4,7},{5,4},{6,5},{7,6},{8,11},{9,8},{10,9... | collective-permute-start | bytes 786440 | tf_op jit(solution)/shard_map/ppermute | solution.py:20
  156.3 38.3 %collective-permute-start.6 = (bf16[128,1024]{1,0:T(8,128)(2,1)}, bf16[128,1024]{1,0:T(8,128)(2,1)}, u32[]{:S(2)}, u32[]{:S(2)}) collective-permute-start(bf16[128,1024]{1,0:T(8,128)(2,1)} %get-tuple-element.28), channel_id=1, source_target_pairs={{0,6},{1,7},{2,4},{3,5},{4,2},{5,3},{6,0},{7,1},{8,14},{9,15},{10,... | collective-permute-start | bytes 786440 | tf_op jit(solution)/shard_map/ppermute | solution.py:20
  160.9 32.0 %collective-permute-start.5 = (bf16[128,1024]{1,0:T(8,128)(2,1)}, bf16[128,1024]{1,0:T(8,128)(2,1)}, u32[]{:S(2)}, u32[]{:S(2)}) collective-permute-start(bf16[128,1024]{1,0:T(8,128)(2,1)} %get-tuple-element.28), channel_id=1, source_target_pairs={{0,7},{1,4},{2,5},{3,6},{4,3},{5,0},{6,1},{7,2},{8,15},{9,12},{10,... | collective-permute-start | bytes 786440 | tf_op jit(solution)/shard_map/ppermute | solution.py:20
  163.5 24.3 %collective-permute-start.3 = (bf16[128,1024]{1,0:T(8,128)(2,1)}, bf16[128,1024]{1,0:T(8,128)(2,1)S(1)}, u32[]{:S(2)}, u32[]{:S(2)}) collective-permute-start(bf16[128,1024]{1,0:T(8,128)(2,1)} %get-tuple-element.28), channel_id=1, source_target_pairs={{0,4},{1,5},{2,6},{3,7},{4,0},{5,1},{6,2},{7,3},{8,12},{9,13},{10,... | collective-permute-start | bytes 786440 | tf_op jit(solution)/shard_map/ppermute | solution.py:20
  220.2 21.5 %collective-permute-start.13 = (bf16[128,1024]{1,0:T(8,128)(2,1)S(1)}, bf16[128,1024]{1,0:T(8,128)(2,1)S(1)}, u32[]{:S(2)}, u32[]{:S(2)}) collective-permute-start(bf16[128,1024]{1,0:T(8,128)(2,1)S(1)} %get-tuple-element.41), channel_id=1, source_target_pairs={{0,6},{1,7},{2,4},{3,5},{4,2},{5,3},{6,0},{7,1},{8,14},{9,15},{10,... | collective-permute-start | bytes 786440 | tf_op jit(solution)/shard_map/ppermute | solution.py:20
  224.9 21.7 %collective-permute-start.21 = (bf16[128,1024]{1,0:T(8,128)(2,1)S(1)}, bf16[128,1024]{1,0:T(8,128)(2,1)S(1)}, u32[]{:S(2)}, u32[]{:S(2)}) collective-permute-start(bf16[128,1024]{1,0:T(8,128)(2,1)S(1)} %get-tuple-element.33), channel_id=1, source_target_pairs={{0,3},{1,0},{2,1},{3,2},{4,7},{5,4},{6,5},{7,6},{8,11},{9,8},{10,9... | collective-permute-start | bytes 786440 | tf_op jit(solution)/shard_map/ppermute | solution.py:20
  225.6 22.4 %collective-permute-start.27 = (bf16[128,1024]{1,0:T(8,128)(2,1)S(1)}, bf16[128,1024]{1,0:T(8,128)(2,1)S(1)}, u32[]{:S(2)}, u32[]{:S(2)}) collective-permute-start(bf16[128,1024]{1,0:T(8,128)(2,1)S(1)} %get-tuple-element.34), channel_id=1, source_target_pairs={{0,6},{1,7},{2,4},{3,5},{4,2},{5,3},{6,0},{7,1},{8,14},{9,15},{10,... | collective-permute-start | bytes 786440 | tf_op jit(solution)/shard_map/ppermute | solution.py:20
  226.7 28.2 %collective-permute-start.26 = (bf16[128,1024]{1,0:T(8,128)(2,1)}, bf16[128,1024]{1,0:T(8,128)(2,1)}, u32[]{:S(2)}, u32[]{:S(2)}) collective-permute-start(bf16[128,1024]{1,0:T(8,128)(2,1)} %get-tuple-element.35), channel_id=1, source_target_pairs={{0,5},{1,6},{2,7},{3,4},{4,1},{5,2},{6,3},{7,0},{8,13},{9,14},{10,... | collective-permute-start | bytes 786440 | tf_op jit(solution)/shard_map/ppermute | solution.py:20
  235.7 19.7 %collective-permute-start.25 = (bf16[128,1024]{1,0:T(8,128)(2,1)}, bf16[128,1024]{1,0:T(8,128)(2,1)}, u32[]{:S(2)}, u32[]{:S(2)}) collective-permute-start(bf16[128,1024]{1,0:T(8,128)(2,1)} %get-tuple-element.36), channel_id=1, source_target_pairs={{0,7},{1,4},{2,5},{3,6},{4,3},{5,0},{6,1},{7,2},{8,15},{9,12},{10,... | collective-permute-start | bytes 786440 | tf_op jit(solution)/shard_map/ppermute | solution.py:20
  267.7 58.2 %collective-permute-start.34 = (bf16[256,1024]{1,0:T(8,128)(2,1)}, bf16[256,1024]{1,0:T(8,128)(2,1)}, u32[]{:S(2)}, u32[]{:S(2)}) collective-permute-start(bf16[256,1024]{1,0:T(8,128)(2,1)} %dynamic-slice_convert_fusion.1), channel_id=1, source_target_pairs={{0,8},{8,0},{1,9},{9,1},{2,10},{10,2},{3,11},{11,3},{4,12},{12,4},... | collective-permute-start | bytes 1572872 | tf_op jit(solution)/shard_map/ppermute | solution.py:35
  271.6 56.4 %collective-permute-start.32 = (bf16[64,4096]{1,0:T(8,128)(2,1)}, bf16[64,4096]{1,0:T(8,128)(2,1)}, u32[]{:S(2)}, u32[]{:S(2)}) collective-permute-start(bf16[64,4096]{1,0:T(8,128)(2,1)} %copy.202), channel_id=1, source_target_pairs={{0,8},{8,0},{1,9},{9,1},{2,10},{10,2},{3,11},{11,3},{4,12},{12,4},... | collective-permute-start | bytes 1572872 | tf_op jit(solution)/shard_map/ppermute | solution.py:35
  290.2 97.1 %reduce-scatter.11.cloned.1.call-start = ((), (), s32[]{:S(2)}) async-start(), calls=%async_computation.22 | async-start | bytes 589824 | tf_op jit(solution)/shard_map/reduce_scatter | solution.py:297
  294.2 57.7 %collective-permute-start.30 = (bf16[64,8,1024]{2,0,1:T(8,128)(2,1)}, bf16[64,8,1024]{2,0,1:T(8,128)(2,1)}, u32[]{:S(2)}, u32[]{:S(2)}) collective-permute-start(bf16[64,8,1024]{2,0,1:T(8,128)(2,1)} %fusion.23), channel_id=1, source_target_pairs={{0,8},{8,0},{1,9},{9,1},{2,10},{10,2},{3,11},{11,3},{4,12},{12,4},... | collective-permute-start | bytes 3145736 | tf_op jit(solution)/shard_map/ppermute | solution.py:35
  363.7 77.7 %reduce-scatter.5.cloned.1.call-start = ((), (), s32[]{:S(2)}) async-start(), calls=%async_computation.19 | async-start | bytes 442368 | tf_op jit(solution)/shard_map/reduce_scatter | solution.py:297
  375.7 131.6 %all-to-all-start.7 = ((bf16[8,128,1024]{2,1,0:T(8,128)(2,1)}), bf16[8,128,1024]{2,1,0:T(8,128)(2,1)S(1)}, u32[]{:S(2)}, u32[]{:S(2)}) async-start(bf16[8,128,1024]{2,1,0:T(8,128)(2,1)} %bitcast.216), calls=%async_computation.7 | async-start | bytes 4194304 | tf_op jit(solution)/shard_map/all_to_all | solution.py:39
  383.0 89.3 %reduce-scatter.9.cloned.1.call-start = ((), (), s32[]{:S(2)}) async-start(), calls=%async_computation.21 | async-start | bytes 589824 | tf_op jit(solution)/shard_map/reduce_scatter | solution.py:297
  384.9 153.7 %reduce-scatter.7.cloned.1.call-start = ((), (), s32[]{:S(2)}) async-start(), calls=%async_computation.20 | async-start | bytes 147456 | tf_op jit(solution)/shard_map/reduce_scatter | solution.py:297
  433.7 69.9 %collective-permute-start.35 = (bf16[256,1024]{1,0:T(8,128)(2,1)}, bf16[256,1024]{1,0:T(8,128)(2,1)}, u32[]{:S(2)}, u32[]{:S(2)}) collective-permute-start(bf16[256,1024]{1,0:T(8,128)(2,1)} %all_gather.15), channel_id=1, source_target_pairs={{0,8},{8,0},{1,9},{9,1},{2,10},{10,2},{3,11},{11,3},{4,12},{12,4},... | collective-permute-start | bytes 1572872 | tf_op jit(solution)/shard_map/ppermute | solution.py:35
  466.2 51.4 %collective-permute-start.29 = (bf16[64,3072]{1,0:T(8,128)(2,1)}, bf16[64,3072]{1,0:T(8,128)(2,1)}, u32[]{:S(2)}, u32[]{:S(2)}) collective-permute-start(bf16[64,3072]{1,0:T(8,128)(2,1)} %all_gather.12), channel_id=1, source_target_pairs={{0,8},{8,0},{1,9},{9,1},{2,10},{10,2},{3,11},{11,3},{4,12},{12,4},... | collective-permute-start | bytes 1179656 | tf_op jit(solution)/shard_map/ppermute | solution.py:35
  497.5 95.6 %collective-permute-start.33 = (bf16[64,4096]{1,0:T(8,128)(2,1)}, bf16[64,4096]{1,0:T(8,128)(2,1)}, u32[]{:S(2)}, u32[]{:S(2)}) collective-permute-start(bf16[64,4096]{1,0:T(8,128)(2,1)} %all_gather.14), channel_id=1, source_target_pairs={{0,8},{8,0},{1,9},{9,1},{2,10},{10,2},{3,11},{11,3},{4,12},{12,4},... | collective-permute-start | bytes 1572872 | tf_op jit(solution)/shard_map/ppermute | solution.py:35
  510.3 62.6 %all-to-all-start.8 = ((f32[8,1,7168]{2,1,0:T(1,128)}), f32[8,1,7168]{2,1,0:T(1,128)S(1)}, u32[]{:S(2)}, u32[]{:S(2)}) async-start(f32[8,1,7168]{2,1,0:T(1,128)} %broadcast_in_dim.49), calls=%async_computation.8 | async-start | bytes 458752 | tf_op jit(solution)/shard_map/all_to_all | solution.py:39
  560.7 35.3 %collective-permute-start.31 = (bf16[64,1024]{1,0:T(8,128)(2,1)S(1)}, bf16[64,1024]{1,0:T(8,128)(2,1)S(1)}, u32[]{:S(2)}, u32[]{:S(2)}) collective-permute-start(bf16[64,1024]{1,0:T(8,128)(2,1)S(1)} %all_gather.13), channel_id=1, source_target_pairs={{0,8},{8,0},{1,9},{9,1},{2,10},{10,2},{3,11},{11,3},{4,12},{12,4},... | collective-permute-start | bytes 393224 | tf_op jit(solution)/shard_map/ppermute | solution.py:35
  (68 other events, 1004.7 us)
Sparse Core Ops, SparseCore 0:
  328.1 31.4 reduce-scatter.10
  367.0 38.4 reduce-scatter.4
  408.5 36.9 reduce-scatter.8
  507.4 31.2 reduce-scatter.6
